TPU v7x, 32 devices: a whole 2x2x4 slice. The times are simulated.
32 devices in a mesh: cplx: 2 (over y), row: 4 (over x, core), col: 4 (over z).
Axes of the slice: x: 2, y: 2, z: 4, core: 2. Of those that a mesh axis runs over, the one named last changes fastest.
Arguments:
- pair_rep: bfloat16 [128, 64, 128], P(('cplx', 'row'), 'col'), parts along dimension 0, may hold values from -6 to 6
- pair_mask: int32 [128, 64], P(('cplx', 'row'), 'col'), parts along dimension 0, may hold values from 0 to 1, as said below
- norm_gain: float32 [128], replicated, may hold values from 0.5 to 1.5
- norm_bias: float32 [128], replicated, may hold values from -3 to 3
- proj_weight: bfloat16 [128, 640], replicated, may hold values from -0.5 to 0.5
- out_gain: float32 [128], replicated, may hold values from 0.5 to 1.5
- out_bias: float32 [128], replicated, may hold values from -3 to 3
- out_weight: bfloat16 [128, 128], replicated, may hold values from -0.5 to 0.5
Outputs:
- update: bfloat16 [128, 64, 128], P(('cplx', 'row', 'col')), parts along dimension 0
There are 2 independent parts, one for each index of `cplx`. A program takes and returns all parts, laid end to end along the dimension named above; an argument that names none is the same for every part. Nothing has to cross between parts.
Inputs may be any that keep to these rules, and one draw needn't show every extreme that they name: pair_mask[i, j] = v[i] v[j] for a 0/1 validity v of the tokens.
All inputs are finite; a program needn't handle non-finite values.
Results may differ from a plain program's by a relative error of at most 0.0085.
Values may be sent and summed in bfloat16 or wider, within the bound.
A program may use at most 128 MiB of HBM per device.

v0:
```python
import jax
import jax.numpy as jnp
from jax import lax
from jax.sharding import PartitionSpec as P


def normalize(values, scale_gain, shift_bias):
    average = jnp.mean(values, axis=-1, keepdims=True)
    centered = values - average
    variance = jnp.mean(centered * centered, axis=-1, keepdims=True)
    return centered * lax.rsqrt(variance + 1e-05) * scale_gain + shift_bias


def finish(mixed_sum, gating, out_gain, out_bias, out_weight):
    channels = mixed_sum.shape[2]
    normed_out = normalize(mixed_sum, out_gain, out_bias).astype(jnp.bfloat16)
    lifted = jnp.dot(
        normed_out.reshape(-1, channels), out_weight, preferred_element_type=jnp.float32
    )
    lifted = lifted.reshape(mixed_sum.shape)
    return (gating.astype(jnp.float32) * lifted).astype(jnp.bfloat16)


def remap_rows(tile_update):
    return lax.all_to_all(tile_update, "col", split_axis=0, concat_axis=1, tiled=True)


def on_device(
    pair_rep, pair_mask, norm_gain, norm_bias, proj_weight, out_gain, out_bias, out_weight
):
    channels = pair_rep.shape[2]
    tile_rows = pair_rep.shape[0]
    tile_cols = pair_rep.shape[1]
    normed = normalize(pair_rep.astype(jnp.float32), norm_gain, norm_bias).astype(jnp.bfloat16)
    projected = jnp.dot(
        normed.reshape(-1, channels), proj_weight, preferred_element_type=jnp.float32
    )
    projected = projected.reshape(tile_rows, tile_cols, 5 * channels)
    validity = pair_mask.astype(jnp.float32)[:, :, None]
    left_side = (
        jax.nn.sigmoid(projected[:, :, :channels])
        * projected[:, :, channels : 2 * channels]
        * validity
    ).astype(jnp.bfloat16)
    right_side = (
        jax.nn.sigmoid(projected[:, :, 2 * channels : 3 * channels])
        * projected[:, :, 3 * channels : 4 * channels]
        * validity
    ).astype(jnp.bfloat16)
    gating = jax.nn.sigmoid(projected[:, :, 4 * channels :]).astype(jnp.bfloat16)
    partial_value = jnp.einsum(
        "ikc,jkc->ijc",
        left_side,
        lax.all_gather(right_side, "row", axis=0, tiled=True),
        preferred_element_type=jnp.float32,
    )
    mixed_sum = lax.psum_scatter(partial_value, "col", scatter_dimension=1, tiled=True)
    update = remap_rows(finish(mixed_sum, gating, out_gain, out_bias, out_weight))
    return update


def solution(mesh):
    return jax.shard_map(
        on_device,
        mesh=mesh,
        in_specs=(
            P(("cplx", "row"), "col", None),
            P(("cplx", "row"), "col"),
            P(),
            P(),
            P(),
            P(),
            P(),
            P(),
        ),
        out_specs=P(("cplx", "row", "col"), None, None),
        check_vma=False,
    )
```

profile of v0, /device:TPU:0, one launch (start us, length us, event | category | flops | bytes accessed | tf_op | source)
XLA Modules:
  0.0 69.6 jit_solution(3655905627464885685)
XLA Ops:
  6.5 0.0 copy-start
  6.5 0.0 reduce-scatter.2.cloned.1.call-start
  6.5 0.7 %convert_element_type.31 = f32[16,16]{1,0:T(8,128)S(1)} convert(s32[16,16]{1,0:T(8,128)} %param.9) | non-fusion elementwise | flops 256 | bytes 2048 | tf_op jit(solution)/shard_map/convert_element_type | solution.py:39
  7.3 0.9 %convert_reduce_fusion = f32[16,16]{1,0:T(8,128)S(1)} fusion(bf16[16,16,128]{2,1,0:T(8,128)(2,1)} %param.8), kind=kLoop, calls=%fused_computation.4 | loop fusion | flops 65280 | bytes 66560 | tf_op jit(solution)/shard_map/reduce_sum | solution.py:8
  8.2 1.0 %fusion.5 = f32[16,16]{1,0:T(8,128)S(1)} fusion(bf16[16,16,128]{2,1,0:T(8,128)(2,1)} %param.8, f32[16,16]{1,0:T(8,128)S(1)} %broadcast_multiply_fusion.1), kind=kLoop, calls=%fused_computation.9 | loop fusion | flops 130816 | bytes 67584 | tf_op jit(solution)/shard_map/reduce_sum | solution.py:10
  9.3 0.0 copy-done
  9.3 1.2 %fusion.1 = f32[16,16,640]{2,1,0:T(8,128)S(1)} fusion(bf16[128,640]{1,0:T(8,128)(2,1)S(1)} %copy-done, bf16[16,16,128]{2,1,0:T(8,128)(2,1)} %param.8, f32[128]{0:T(128)} %param.11, f32[128]{0:T(128)} %param.10, f32[16,16]{1,0:T(8,128)S(1)} %add_rsqrt_fusion.1, f32[16,16]{1,0:T(8,128)S(1)} %broadcast_multiply_fusion.1), kind=kOutput, calls=%fused_computation.5 | convolution fusion | flops 42139648 | bytes 887808 | tf_op jit(solution)/shard_map/dot_general | solution.py:35
  10.5 0.0 copy-start.1
  10.5 0.8 %copy-done.1 = f32[16,16,640]{2,1,0:T(8,128)} copy-done((f32[16,16,640]{2,1,0:T(8,128)}, f32[16,16,640]{2,1,0:T(8,128)S(1)}, u32[]{:S(2)}) %copy-start.1) | copy-done | bytes 655384
  11.3 0.1 fusion.10
  11.4 7.2 %all_gather.3 = bf16[64,16,128]{2,1,0:T(8,128)(2,1)S(1)} all-gather(bf16[16,16,128]{2,1,0:T(8,128)(2,1)S(1)} %get-tuple-element.6), channel_id=1, replica_groups=mesh['cplx'=2,'row'=4,'col'=4] {'row'}, dimensions={0}, use_global_device_ids=true | all-gather | bytes 327680 | tf_op jit(solution)/shard_map/all_gather | solution.py:54
  18.6 1.2 %copy.28 = bf16[16,16,128]{1,0,2:T(8,128)(2,1)} copy(bf16[16,16,128]{2,1,0:T(8,128)(2,1)S(1)} %get-tuple-element.5) | data formatting | bytes 131072 | tf_op jit(solution)/shard_map/convert_element_type | solution.py:44
  19.8 2.9 %copy.27 = bf16[64,16,128]{1,0,2:T(8,128)(2,1)S(1)} copy(bf16[64,16,128]{2,1,0:T(8,128)(2,1)S(1)} %all_gather.3) | data formatting | bytes 524288 | tf_op jit(solution)/shard_map/all_gather | solution.py:54
  22.7 2.2 %convolution_bitcast_fusion = f32[16,64,128]{1,0,2:T(8,128)S(1)} fusion(bf16[64,16,128]{1,0,2:T(8,128)(2,1)S(1)} %copy.27, bf16[16,16,128]{1,0,2:T(8,128)(2,1)} %copy.28), kind=kOutput, calls=%fused_computation | convolution fusion | flops 4194304 | bytes 851968 | tf_op jit(solution)/shard_map/ikc,jkc->ijc/dot_general | solution.py:51
  25.0 0.0 copy-start.2
  25.0 0.0 copy-start.4
  25.0 1.3 %copy.29 = f32[16,64,128]{2,0,1:T(8,128)} copy(f32[16,64,128]{1,0,2:T(8,128)S(1)} %convolution_bitcast_fusion) | data formatting | bytes 1048576 | tf_op jit(solution)/shard_map/ikc,jkc->ijc/transpose | solution.py:51
  26.3 0.0 reduce-scatter.2.cloned.1.call-update
  26.3 23.1 %reduce-scatter.2.cloned.1.call-done = f32[16,16,128]{2,0,1:T(8,128)} async-done(((f32[16,64,128]{2,0,1:T(8,128)}), f32[16,16,128]{2,0,1:T(8,128)}) %reduce-scatter.2.cloned.1.call-update) | async-done | bytes 131088 | tf_op jit(solution)/shard_map/reduce_scatter | solution.py:57
  49.5 1.0 %reduce_sum.38 = f32[16,16]{0,1:T(8,128)S(1)} reduce(f32[16,16,128]{2,0,1:T(8,128)} %reduce-scatter.2.cloned.1.call-done, f32[]{:T(128)} %constant.9.clone.1), dimensions={2}, to_apply=%region_3.0 | reduce | flops 32512 | bytes 132100 | tf_op jit(solution)/shard_map/reduce_sum | solution.py:8
  50.5 0.1 copy.30
  50.5 0.1 copy.31
  50.6 1.1 %multiply_reduce_fusion = f32[16,16]{0,1:T(8,128)S(1)} fusion(f32[16,16,128]{2,0,1:T(8,128)} %reduce-scatter.2.cloned.1.call-done, f32[16,16]{0,1:T(8,128)S(1)} %copy.31), kind=kLoop, calls=%fused_computation.32 | loop fusion | flops 98048 | bytes 133120 | tf_op jit(solution)/shard_map/reduce_sum | solution.py:10
  51.7 0.1 copy.32
  51.8 0.1 copy.33
  51.9 0.0 copy-done.2
  51.9 0.0 copy-done.3
  51.9 1.0 %add_convert_fusion = bf16[16,16,128]{2,0,1:T(8,128)(2,1)S(1)} fusion(f32[16,16,128]{2,0,1:T(8,128)} %reduce-scatter.2.cloned.1.call-done, f32[128]{0:T(128)S(1)} %copy-done.2, f32[128]{0:T(128)S(1)} %copy-done.3, f32[16,16]{0,1:T(8,128)S(1)} %copy.33, f32[16,16]{0,1:T(8,128)S(1)} %copy.31), kind=kLoop, calls=%fused_computation.31 | loop fusion | flops 163840 | bytes 199680 | tf_op jit(solution)/shard_map/convert_element_type | solution.py:16
  52.9 0.0 copy-done.4
  53.0 1.1 %fusion = bf16[16,16,128]{2,1,0:T(8,128)(2,1)S(1)} fusion(f32[16,16,640]{2,1,0:T(8,128)} %copy-done.1, bf16[16,16,128]{2,0,1:T(8,128)(2,1)S(1)} %add_convert_fusion, bf16[128,128]{1,0:T(8,128)(2,1)S(1)} %copy-done.4), kind=kOutput, calls=%fused_computation.2 | convolution fusion | flops 8617984 | bytes 294912 | tf_op jit(solution)/shard_map/dot_general | solution.py:17
  54.0 8.1 %all_to_all.18 = bf16[16,16,128]{2,1,0:T(8,128)(2,1)S(1)} all-to-all(bf16[16,16,128]{2,1,0:T(8,128)(2,1)S(1)} %fusion), channel_id=1, replica_groups=mesh['cplx'=2,'row'=4,'col'=4] {'col'}, dimensions={0} | all-to-all | bytes 131072 | tf_op jit(solution)/shard_map/all_to_all | solution.py:25
  62.1 0.6 copy.35
  (5 shorter events, 0.0 us)
Async XLA Ops:
  6.5 2.8 %copy-start = (bf16[128,640]{1,0:T(8,128)(2,1)S(1)}, bf16[128,640]{1,0:T(8,128)(2,1)}, u32[]{:S(2)}) copy-start(bf16[128,640]{1,0:T(8,128)(2,1)} %param.12) | copy-start | bytes 491524
  6.5 42.9 %reduce-scatter.2.cloned.1.call-start = ((), (), s32[]{:S(2)}) async-start(), calls=%async_computation.2 | async-start | bytes 655360 | tf_op jit(solution)/shard_map/reduce_scatter | solution.py:57
  10.5 0.8 %copy-start.1 = (f32[16,16,640]{2,1,0:T(8,128)}, f32[16,16,640]{2,1,0:T(8,128)S(1)}, u32[]{:S(2)}) copy-start(f32[16,16,640]{2,1,0:T(8,128)S(1)} %fusion.1) | copy-start | bytes 1966084
  25.0 26.9 %copy-start.2 = (f32[128]{0:T(128)S(1)}, f32[128]{0:T(128)}, u32[]{:S(2)}) copy-start(f32[128]{0:T(128)} %param.14) | copy-start | bytes 1540
  25.0 26.9 %copy-start.3 = (f32[128]{0:T(128)S(1)}, f32[128]{0:T(128)}, u32[]{:S(2)}) copy-start(f32[128]{0:T(128)} %param.13) | copy-start | bytes 1540
  25.0 28.0 %copy-start.4 = (bf16[128,128]{1,0:T(8,128)(2,1)S(1)}, bf16[128,128]{1,0:T(8,128)(2,1)}, u32[]{:S(2)}) copy-start(bf16[128,128]{1,0:T(8,128)(2,1)} %param.15) | copy-start | bytes 98308
Sparse Core Ops, SparseCore 0:
  26.5 22.9 reduce-scatter.1
where the time goes:
time: 70 us; the launch traced here: 69.6 us
  waiting for transfers between devices  23.1 us (33%)
  blocking collectives  15.3 us (22%)
  between operations  13.5 us (19%)
  local copies, waits for them, and re-layouts  7.23 us (10%)
  other arithmetic  5.98 us (9%)
  matrix products  4.44 us (6%)
    reduce_scatter x1, waiting for transfers between devices, on_device(): lax.psum_scatter(partial_value, 'col', scatter_dimension=1, tiled=True)  23.1 us
    all_to_all x1, blocking collectives, remap_rows(): lax.all_to_all(tile_update, 'col', split_axis=0, concat_axis=1, tiled=True)  8.11 us
    all_gather x1, blocking collectives, on_device(): lax.all_gather(right_side, 'row', axis=0, tiled=True)  7.19 us
    all_gather x1, local copies, waits for them, and re-layouts, on_device(): lax.all_gather(right_side, 'row', axis=0, tiled=True)  2.95 us
    dot_general x1, matrix products, on_device(): jnp.einsum('ikc,jkc->ijc', left_side, lax.all_gather(right_side, 'row', a...  2.22 us
    reduce_sum x2, other arithmetic, normalize(): variance = jnp.mean(centered * centered, axis=-1, keepdims=True)  2.12 us
    reduce_sum x2, other arithmetic, normalize(): average = jnp.mean(values, axis=-1, keepdims=True)  1.95 us
  transfers between devices with their start and end apart: 1, of which 1 were waited for; matrix products, arithmetic and copies ran while one was open for 0% of the time, Pallas kernels for 0%

commit v1 on v0

v1 whole, which is shorter than its diff:
```python
import functools

import jax
import jax.numpy as jnp
from jax import lax
from jax.experimental import pallas as pl
from jax.experimental.pallas import tpu as pltpu
from jax.sharding import PartitionSpec as P

MESH = pl.DeviceIdType.MESH
F32, BF16 = jnp.float32, jnp.bfloat16


def normalize(values, scale_gain, shift_bias):
    average = jnp.mean(values, axis=-1, keepdims=True)
    centered = values - average
    variance = jnp.mean(centered * centered, axis=-1, keepdims=True)
    return centered * lax.rsqrt(variance + 1e-05) * scale_gain + shift_bias


def finish(mixed_sum, gating, out_gain, out_bias, out_weight):
    channels = mixed_sum.shape[2]
    normed_out = normalize(mixed_sum, out_gain, out_bias).astype(BF16)
    lifted = jnp.dot(
        normed_out.reshape(-1, channels), out_weight, preferred_element_type=F32
    )
    lifted = lifted.reshape(mixed_sum.shape)
    return (gating.astype(F32) * lifted).astype(BF16)


def general_form(
    pair_rep, pair_mask, norm_gain, norm_bias, proj_weight, out_gain, out_bias, out_weight
):
    rows, cols, channels = pair_rep.shape
    normed = normalize(pair_rep.astype(F32), norm_gain, norm_bias).astype(BF16)
    projected = jnp.dot(normed.reshape(-1, channels), proj_weight, preferred_element_type=F32)
    projected = projected.reshape(rows, cols, 5 * channels)
    validity = pair_mask.astype(F32)[:, :, None]
    p = [projected[:, :, n * channels : (n + 1) * channels] for n in range(5)]
    left_side = (jax.nn.sigmoid(p[0]) * p[1] * validity).astype(BF16)
    right_side = (jax.nn.sigmoid(p[2]) * p[3] * validity).astype(BF16)
    gating = jax.nn.sigmoid(p[4]).astype(BF16)
    partial_value = jnp.einsum(
        "ikc,jkc->ijc",
        left_side,
        lax.all_gather(right_side, "row", axis=0, tiled=True),
        preferred_element_type=F32,
    )
    mixed_sum = lax.psum_scatter(partial_value, "col", scatter_dimension=1, tiled=True)
    update = finish(mixed_sum, gating, out_gain, out_bias, out_weight)
    return lax.all_to_all(update, "col", split_axis=0, concat_axis=1, tiled=True)


def kernel(
    sizes,
    x_hbm, mask_hbm, gain_hbm, bias_hbm, w_hbm, ogain_hbm, obias_hbm, ow_hbm,
    out_ref,
    x_v, mask_v, gain_v, bias_v, w_v, ogain_v, obias_v, ow_v,
    right_f, left_f, right_b, x_g, gate, part_s, part_r, part_own,
    in_sem, right_ss, right_rs, x_ss, x_rs, part_ss, part_rs,
):
    R, S, ti, tk, C = sizes
    so = ti // S
    row, col = lax.axis_index("row"), lax.axis_index("col")

    barrier = pltpu.get_barrier_semaphore()
    for off in range(1, R):
        pl.semaphore_signal(barrier, inc=1, device_id={"row": row ^ off}, device_id_type=MESH)
    for off in range(1, S):
        pl.semaphore_signal(barrier, inc=1, device_id={"col": col ^ off}, device_id_type=MESH)

    loads = [
        pltpu.make_async_copy(src, dst, in_sem.at[n])
        for n, (src, dst) in enumerate(
            [
                (x_hbm, x_v), (mask_hbm, mask_v), (gain_hbm, gain_v), (bias_hbm, bias_v),
                (w_hbm, w_v), (ogain_hbm, ogain_v), (obias_hbm, obias_v), (ow_hbm, ow_v),
                (x_hbm.at[pl.ds(col * so, so)], x_g.at[0]),
            ]
        )
    ]
    for load in loads:
        load.start()
    for load in loads:
        load.wait()

    gain, bias = gain_v[...].reshape(1, C), bias_v[...].reshape(1, C)
    validity = mask_v[...].astype(F32)[:, :, None]
    step = max(1, 64 // tk)
    for i0 in range(0, ti, step):
        x = x_v[i0 : i0 + step].astype(F32).reshape(step * tk, C)
        normed = normalize(x, gain, bias).astype(BF16)
        p = jnp.dot(normed, w_v[:, : 4 * C], preferred_element_type=F32)
        valid = validity[i0 : i0 + step].reshape(step * tk, 1)
        left = jax.nn.sigmoid(p[:, :C]) * p[:, C : 2 * C] * valid
        right = jax.nn.sigmoid(p[:, 2 * C : 3 * C]) * p[:, 3 * C :] * valid
        left_f[i0 * tk : (i0 + step) * tk] = left.astype(BF16).astype(F32)
        right_f[i0 * tk : (i0 + step) * tk] = right
    for k in range(tk):
        right_b[0, k] = right_f[pl.ds(k, ti, stride=tk), :].astype(BF16)

    pl.semaphore_wait(barrier, R + S - 2)

    right_copies = {
        off: pltpu.make_async_remote_copy(
            src_ref=right_b.at[0], dst_ref=right_b.at[off],
            send_sem=right_ss.at[off], recv_sem=right_rs.at[off],
            device_id={"row": row ^ off}, device_id_type=MESH,
        )
        for off in range(1, R)
    }
    x_copies = {
        off: pltpu.make_async_remote_copy(
            src_ref=x_hbm.at[pl.ds((col ^ off) * so, so)], dst_ref=x_g.at[off],
            send_sem=x_ss.at[off], recv_sem=x_rs.at[off],
            device_id={"col": col ^ off}, device_id_type=MESH,
        )
        for off in range(1, S)
    }
    for off in range(R - 1, 0, -1):
        right_copies[off].start()
    for off in range(S - 1, 0, -1):
        x_copies[off].start()

    part_copies = {
        (off, s): pltpu.make_async_remote_copy(
            src_ref=part_s.at[off, s], dst_ref=part_r.at[off, s],
            send_sem=part_ss.at[off, s], recv_sem=part_rs.at[off, s],
            device_id={"col": col ^ s}, device_id_type=MESH,
        )
        for off in range(R)
        for s in range(1, S)
    }

    def mix(off):
        right = [right_b[off, k].astype(F32) for k in range(tk)]
        for s in list(range(S - 1, -1, -1)):
            base = (col ^ s) * (so * tk)

            def one_row(ii, carry):
                at = base + ii * tk
                sums = [None, None]
                for k in range(tk):
                    term = left_f[pl.ds(at + k, 1), :] * right[k]
                    sums[k % 2] = term if sums[k % 2] is None else sums[k % 2] + term
                total = sums[0] + sums[1]
                if s:
                    part_s[off, s, ii] = total.astype(BF16)
                else:
                    part_own[off, ii] = total
                return carry

            lax.fori_loop(0, so, one_row, 0, unroll=True)
            if s:
                part_copies[off, s].start()

    def gates():
        for off in range(1, S):
            x_copies[off].wait_recv()
        for off in range(S):
            x = x_g[off].astype(F32).reshape(so * tk, C)
            normed = normalize(x, gain, bias).astype(BF16)
            p = jnp.dot(normed, w_v[:, 4 * C :], preferred_element_type=F32)
            g = jax.nn.sigmoid(p).astype(BF16).astype(F32)
            gate[:, pl.ds(pl.multiple_of((col ^ off) * tk, tk), tk), :] = g.reshape(so, tk, C)

    def close(off):
        total = part_own[off]
        for s in range(1, S):
            part_copies[off, s].wait_recv()
            total = total + part_r[off, s].astype(F32)
        total = total.reshape(so * ti, C)
        ogain, obias = ogain_v[...].reshape(1, C), obias_v[...].reshape(1, C)
        normed_out = normalize(total, ogain, obias).astype(BF16)
        lifted = jnp.dot(normed_out, ow_v[...], preferred_element_type=F32)
        at = pl.ds(pl.multiple_of((row ^ off) * ti, ti), ti)
        out_ref[:, at, :] = (gate[:, at, :] * lifted.reshape(so, ti, C)).astype(BF16)

    mix(0)
    for off in range(1, R):
        right_copies[off].wait_recv()
        mix(off)
        if off == 1:
            gates()
    if R == 1:
        gates()
    for off in range(R):
        close(off)

    for copies in (right_copies, x_copies, part_copies):
        for copy in copies.values():
            copy.wait_send()


def kernel_form(R, S, *arguments):
    pair_rep = arguments[0]
    ti, tk, C = pair_rep.shape
    so = ti // S
    vmem, dma = pltpu.VMEM, pltpu.SemaphoreType.DMA
    return pl.pallas_call(
        functools.partial(kernel, (R, S, ti, tk, C)),
        out_shape=jax.ShapeDtypeStruct((so, R * ti, C), BF16),
        in_specs=[pl.BlockSpec(memory_space=pl.ANY)] * 8,
        out_specs=pl.BlockSpec(memory_space=pltpu.VMEM),
        scratch_shapes=[vmem(a.shape, a.dtype) for a in arguments]
        + [
            vmem((ti * tk, C), F32),
            vmem((ti * tk, C), F32),
            vmem((R, tk, ti, C), BF16),
            vmem((S, so, tk, C), BF16),
            vmem((so, S * tk, C), F32),
            vmem((R, S, so, ti, C), BF16),
            vmem((R, S, so, ti, C), BF16),
            vmem((R, so, ti, C), F32),
            dma((9,)), dma((R,)), dma((R,)), dma((S,)), dma((S,)), dma((R, S)), dma((R, S)),
        ],
        compiler_params=pltpu.CompilerParams(
            collective_id=0, has_side_effects=True, vmem_limit_bytes=24 * 2**20
        ),
    )(*arguments)


def solution(mesh):
    R, S = mesh.shape["row"], mesh.shape["col"]

    def on_device(*arguments):
        ti, tk, C = arguments[0].shape
        small = (
            R in (2, 4) and S in (2, 4) and R * ti == S * tk and C == 128
            and ti == 16 and tk == 16
        )
        if small:
            return kernel_form(R, S, *arguments)
        return general_form(*arguments)

    return jax.shard_map(
        on_device,
        mesh=mesh,
        in_specs=(P(("cplx", "row"), "col", None), P(("cplx", "row"), "col"))
        + (P(),) * 6,
        out_specs=P(("cplx", "row", "col"), None, None),
        check_vma=False,
    )
```

time: 70 us -> 21.1 us (0.30)
  waiting for transfers between devices: 23.1 us -> 0 us
  blocking collectives: 15.3 us -> 0 us
  Pallas kernels: 0 us -> 14.3 us
  between operations: 13.5 us -> 0.02 us
  other arithmetic: 5.98 us -> 0 us
  matrix products: 4.44 us -> 0 us
  local copies, waits for them, and re-layouts: 7.23 us -> 6.46 us
    reduce_scatter x1 -> x0, waiting for transfers between devices: 23.1 us -> none  [on_device(): lax.psum_scatter(partial_value, 'col', scatter_dimension=1, tiled=True)]
    pallas_call x0 -> x1, Pallas kernels: none -> 14.3 us  [kernel_form(): pl.pallas_call(functools.partial(kernel, (R, S, ti, tk, C)), out_shape=ja...]
    all_to_all x1 -> x0, blocking collectives: 8.11 us -> none  [remap_rows(): lax.all_to_all(tile_update, 'col', split_axis=0, concat_axis=1, tiled=True)]
    all_gather x1 -> x0, blocking collectives: 7.19 us -> none  [on_device(): lax.all_gather(right_side, 'row', axis=0, tiled=True)]
    unnamed x10 -> x17, local copies, waits for them, and re-layouts: 0.85 us -> 6.46 us
    dot_general x3 -> x0, matrix products: 4.44 us -> none  [the longest x1 2.22 us: on_device(): jnp.einsum('ikc,jkc->ijc', left_side, lax.all_gather(right_side, 'row', a...]
    reduce_sum x4 -> x0, other arithmetic: 4.07 us -> none  [the longest x2 2.12 us: normalize(): variance = jnp.mean(centered * centered, axis=-1, keepdims=True)]
    all_gather x1 -> x0, local copies, waits for them, and re-layouts: 2.95 us -> none  [on_device(): lax.all_gather(right_side, 'row', axis=0, tiled=True)]
  transfers between devices with their start and end apart: 1 -> 0, of which waited for: 1 -> 0; matrix products, arithmetic and copies ran while one was open for 0% -> 0% of each run, Pallas kernels for 0% -> 0%
where the time goes in v1:
time: 21.1 us; the launch traced here: 20.8 us
  Pallas kernels  14.3 us (68%)
  local copies, waits for them, and re-layouts  6.46 us (31%)
    pallas_call x1, Pallas kernels, kernel_form(): pl.pallas_call(functools.partial(kernel, (R, S, ti, tk, C)), out_shape=ja...  14.3 us
    unnamed x17, local copies, waits for them, and re-layouts  6.46 us

profile of v1, /device:TPU:0, one launch (start us, length us, event | category | flops | bytes accessed | tf_op | source)
XLA Modules:
  0.0 20.8 jit_solution(5180732248429139676)
XLA Ops:
  0.0 0.0 copy-start
  0.0 0.9 %copy-done = bf16[128,640]{1,0:T(8,128)(2,1)S(1)} copy-done((bf16[128,640]{1,0:T(8,128)(2,1)S(1)}, bf16[128,640]{1,0:T(8,128)(2,1)}, u32[]{:S(2)}) %copy-start) | copy-done | bytes 163864
  0.9 0.0 copy-start.1
  0.9 0.8 %copy-done.1 = bf16[16,16,128]{2,1,0:T(8,128)(2,1)S(1)} copy-done((bf16[16,16,128]{2,1,0:T(8,128)(2,1)S(1)}, bf16[16,16,128]{2,1,0:T(8,128)(2,1)}, u32[]{:S(2)}) %copy-start.1) | copy-done | bytes 65560
  1.8 0.0 copy-start.2
  1.8 0.8 %copy-done.2 = bf16[128,128]{1,0:T(8,128)(2,1)S(1)} copy-done((bf16[128,128]{1,0:T(8,128)(2,1)S(1)}, bf16[128,128]{1,0:T(8,128)(2,1)}, u32[]{:S(2)}) %copy-start.2) | copy-done | bytes 32792
  2.5 0.0 copy-start.3
  2.5 0.7 %copy-done.3 = s32[16,16]{1,0:T(8,128)S(1)} copy-done((s32[16,16]{1,0:T(8,128)S(1)}, s32[16,16]{1,0:T(8,128)}, u32[]{:S(2)}) %copy-start.3) | copy-done | bytes 1048
  3.2 0.0 copy-start.4
  3.2 0.7 %copy-done.4 = f32[128]{0:T(128)S(1)} copy-done((f32[128]{0:T(128)S(1)}, f32[128]{0:T(128)}, u32[]{:S(2)}) %copy-start.4) | copy-done | bytes 536
  3.9 0.0 copy-start.5
  3.9 0.7 %copy-done.5 = f32[128]{0:T(128)S(1)} copy-done((f32[128]{0:T(128)S(1)}, f32[128]{0:T(128)}, u32[]{:S(2)}) %copy-start.5) | copy-done | bytes 536
  4.5 0.0 copy-start.6
  4.5 0.7 %copy-done.6 = f32[128]{0:T(128)S(1)} copy-done((f32[128]{0:T(128)S(1)}, f32[128]{0:T(128)}, u32[]{:S(2)}) %copy-start.6) | copy-done | bytes 536
  5.2 0.0 copy-start.7
  5.2 0.7 %copy-done.7 = f32[128]{0:T(128)S(1)} copy-done((f32[128]{0:T(128)S(1)}, f32[128]{0:T(128)}, u32[]{:S(2)}) %copy-start.7) | copy-done | bytes 536
  5.8 14.3 %shard_map.82 = bf16[4,64,128]{2,1,0:T(8,128)(2,1)S(1)} custom-call(bf16[16,16,128]{2,1,0:T(8,128)(2,1)S(1)} %copy-done.1, s32[16,16]{1,0:T(8,128)S(1)} %copy-done.3, f32[128]{0:T(128)S(1)} %copy-done.4, f32[128]{0:T(128)S(1)} %copy-done.5, bf16[128,640]{1,0:T(8,128)(2,1)S(1)} %copy-done, f32[128]{0:T(128)S(1)} %copy-done.6, f32[128]{0:T(128)S(1)} %copy-done.7, ...), custom_call_target="tpu_custom_call" | custom-call | tf_op jit(solution)/shard_map/pallas_call | solution.py:200
  20.1 0.6 %copy.10 = bf16[4,64,128]{2,1,0:T(8,128)(2,1)} copy(bf16[4,64,128]{2,1,0:T(8,128)(2,1)S(1)} %shard_map.82) | data formatting | bytes 131072
Async XLA Ops:
  0.0 0.9 %copy-start = (bf16[128,640]{1,0:T(8,128)(2,1)S(1)}, bf16[128,640]{1,0:T(8,128)(2,1)}, u32[]{:S(2)}) copy-start(bf16[128,640]{1,0:T(8,128)(2,1)} %w_hbm.1) | copy-start | bytes 491524
  0.9 0.8 %copy-start.1 = (bf16[16,16,128]{2,1,0:T(8,128)(2,1)S(1)}, bf16[16,16,128]{2,1,0:T(8,128)(2,1)}, u32[]{:S(2)}) copy-start(bf16[16,16,128]{2,1,0:T(8,128)(2,1)} %x_hbm.1) | copy-start | bytes 196612
  1.8 0.8 %copy-start.2 = (bf16[128,128]{1,0:T(8,128)(2,1)S(1)}, bf16[128,128]{1,0:T(8,128)(2,1)}, u32[]{:S(2)}) copy-start(bf16[128,128]{1,0:T(8,128)(2,1)} %ow_hbm.1) | copy-start | bytes 98308
  2.5 0.7 %copy-start.3 = (s32[16,16]{1,0:T(8,128)S(1)}, s32[16,16]{1,0:T(8,128)}, u32[]{:S(2)}) copy-start(s32[16,16]{1,0:T(8,128)} %mask_hbm.1) | copy-start | bytes 3076
  3.2 0.7 %copy-start.4 = (f32[128]{0:T(128)S(1)}, f32[128]{0:T(128)}, u32[]{:S(2)}) copy-start(f32[128]{0:T(128)} %gain_hbm.1) | copy-start | bytes 1540
  3.9 0.7 %copy-start.5 = (f32[128]{0:T(128)S(1)}, f32[128]{0:T(128)}, u32[]{:S(2)}) copy-start(f32[128]{0:T(128)} %bias_hbm.1) | copy-start | bytes 1540
  4.5 0.7 %copy-start.6 = (f32[128]{0:T(128)S(1)}, f32[128]{0:T(128)}, u32[]{:S(2)}) copy-start(f32[128]{0:T(128)} %ogain_hbm.1) | copy-start | bytes 1540
  5.2 0.7 %copy-start.7 = (f32[128]{0:T(128)S(1)}, f32[128]{0:T(128)}, u32[]{:S(2)}) copy-start(f32[128]{0:T(128)} %obias_hbm.1) | copy-start | bytes 1540

commit v2 on v1

--- a/solution.py
+++ b/solution.py
@@ -81,6 +81,17 @@
     ]
     for load in loads:
         load.start()
+    pl.semaphore_wait(barrier, R + S - 2)
+    x_copies = {
+        off: pltpu.make_async_remote_copy(
+            src_ref=x_hbm.at[pl.ds((col ^ off) * so, so)], dst_ref=x_g.at[off],
+            send_sem=x_ss.at[off], recv_sem=x_rs.at[off],
+            device_id={"col": col ^ off}, device_id_type=MESH,
+        )
+        for off in range(1, S)
+    }
+    for off in range(S - 1, 0, -1):
+        x_copies[off].start()
     for load in loads:
         load.wait()
 
@@ -99,8 +110,6 @@
     for k in range(tk):
         right_b[0, k] = right_f[pl.ds(k, ti, stride=tk), :].astype(BF16)
 
-    pl.semaphore_wait(barrier, R + S - 2)
-
     right_copies = {
         off: pltpu.make_async_remote_copy(
             src_ref=right_b.at[0], dst_ref=right_b.at[off],
@@ -109,18 +118,8 @@
         )
         for off in range(1, R)
     }
-    x_copies = {
-        off: pltpu.make_async_remote_copy(
-            src_ref=x_hbm.at[pl.ds((col ^ off) * so, so)], dst_ref=x_g.at[off],
-            send_sem=x_ss.at[off], recv_sem=x_rs.at[off],
-            device_id={"col": col ^ off}, device_id_type=MESH,
-        )
-        for off in range(1, S)
-    }
     for off in range(R - 1, 0, -1):
         right_copies[off].start()
-    for off in range(S - 1, 0, -1):
-        x_copies[off].start()
 
     part_copies = {
         (off, s): pltpu.make_async_remote_copy(
@@ -215,7 +214,7 @@
             dma((9,)), dma((R,)), dma((R,)), dma((S,)), dma((S,)), dma((R, S)), dma((R, S)),
         ],
         compiler_params=pltpu.CompilerParams(
-            collective_id=0, has_side_effects=True, vmem_limit_bytes=24 * 2**20
+            collective_id=0, has_side_effects=True, vmem_limit_bytes=56 * 2**20
         ),
     )(*arguments)
 

time: 21.1 us -> 16.8 us (0.80); the launches traced: 20.8 us -> 16.7 us
  local copies, waits for them, and re-layouts: 6.46 us -> 1.47 us
  Pallas kernels: 14.3 us -> 15.2 us
    unnamed x17 -> x1, local copies, waits for them, and re-layouts: 6.46 us -> 1.47 us
    pallas_call x1, Pallas kernels: 14.3 us -> 15.2 us  [kernel_form(): pl.pallas_call(functools.partial(kernel, (R, S, ti, tk, C)), out_shape=ja...]
where the time goes in v2:
time: 16.8 us; the launch traced here: 16.7 us
  Pallas kernels  15.2 us (90%)
  local copies, waits for them, and re-layouts  1.47 us (9%)
    pallas_call x1, Pallas kernels, kernel_form(): pl.pallas_call(functools.partial(kernel, (R, S, ti, tk, C)), out_shape=ja...  15.2 us
    unnamed x1, local copies, waits for them, and re-layouts  1.47 us

profile of v2, /device:TPU:0, one launch (start us, length us, event | category | flops | bytes accessed | tf_op | source)
XLA Modules:
  0.0 16.7 jit_solution(16943820975477544752)
XLA Ops:
  0.0 15.2 %shard_map.82 = bf16[4,64,128]{2,1,0:T(8,128)(2,1)} custom-call(bf16[16,16,128]{2,1,0:T(8,128)(2,1)} %x_hbm.1, s32[16,16]{1,0:T(8,128)} %mask_hbm.1, f32[128]{0:T(128)} %gain_hbm.1, f32[128]{0:T(128)} %bias_hbm.1, bf16[128,640]{1,0:T(8,128)(2,1)} %w_hbm.1, f32[128]{0:T(128)} %ogain_hbm.1, f32[128]{0:T(128)} %obias_hbm.1, bf16[128,128]{1,0:T(8,128)(2,1)} %ow_hbm.1), custom_call_target="tpu_custom_call" | custom-call | tf_op jit(solution)/shard_map/pallas_call | solution.py:199
  15.2 1.5 %copy.10 = bf16[4,64,128]{2,1,0:T(8,128)(2,1)} copy(bf16[4,64,128]{2,1,0:T(8,128)(2,1)} %shard_map.82) | data formatting | bytes 131072

commit v3 on v2

--- a/solution.py
+++ b/solution.py
@@ -79,8 +79,8 @@
             ]
         )
     ]
-    for load in loads:
-        load.start()
+    for n in (4, 0, 1, 2, 3, 8, 5, 6, 7):
+        loads[n].start()
     pl.semaphore_wait(barrier, R + S - 2)
     x_copies = {
         off: pltpu.make_async_remote_copy(
@@ -92,7 +92,7 @@
     }
     for off in range(S - 1, 0, -1):
         x_copies[off].start()
-    for load in loads:
+    for load in loads[:5]:
         load.wait()
 
     gain, bias = gain_v[...].reshape(1, C), bias_v[...].reshape(1, C)
@@ -118,7 +118,7 @@
         )
         for off in range(1, R)
     }
-    for off in range(R - 1, 0, -1):
+    for off in range(1, R):
         right_copies[off].start()
 
     part_copies = {
@@ -154,6 +154,7 @@
                 part_copies[off, s].start()
 
     def gates():
+        loads[8].wait()
         for off in range(1, S):
             x_copies[off].wait_recv()
         for off in range(S):
@@ -183,6 +184,8 @@
             gates()
     if R == 1:
         gates()
+    for load in loads[5:8]:
+        load.wait()
     for off in range(R):
         close(off)
 

time: 16.8 us -> 17 us (1.012)
  no operation moved by 1% of the time
where the time goes in v3:
time: 17 us; the launch traced here: 16.8 us
  Pallas kernels  15.3 us (90%)
  local copies, waits for them, and re-layouts  1.47 us (9%)
    pallas_call x1, Pallas kernels, kernel_form(): pl.pallas_call(functools.partial(kernel, (R, S, ti, tk, C)), out_shape=ja...  15.3 us
    unnamed x1, local copies, waits for them, and re-layouts  1.47 us

profile of v3, /device:TPU:0, one launch (start us, length us, event | category | flops | bytes accessed | tf_op | source)
XLA Modules:
  0.0 16.8 jit_solution(17976622402852972504)
XLA Ops:
  0.0 15.3 %shard_map.82 = bf16[4,64,128]{2,1,0:T(8,128)(2,1)} custom-call(bf16[16,16,128]{2,1,0:T(8,128)(2,1)} %x_hbm.1, s32[16,16]{1,0:T(8,128)} %mask_hbm.1, f32[128]{0:T(128)} %gain_hbm.1, f32[128]{0:T(128)} %bias_hbm.1, bf16[128,640]{1,0:T(8,128)(2,1)} %w_hbm.1, f32[128]{0:T(128)} %ogain_hbm.1, f32[128]{0:T(128)} %obias_hbm.1, bf16[128,128]{1,0:T(8,128)(2,1)} %ow_hbm.1), custom_call_target="tpu_custom_call" | custom-call | tf_op jit(solution)/shard_map/pallas_call | solution.py:202
  15.3 1.5 %copy.10 = bf16[4,64,128]{2,1,0:T(8,128)(2,1)} copy(bf16[4,64,128]{2,1,0:T(8,128)(2,1)} %shard_map.82) | data formatting | bytes 131072
